TPU v7x, 256 devices: a whole 4x4x8 slice. The times are simulated.
256 devices in a mesh: dp: 16 (over x_hi, z), tensor: 16 (over x_lo, y, core).
Axes of the slice: x: 4 (x_hi: 2, x_lo: 2; x = x_hi * 2 + x_lo), y: 4, z: 8, core: 2. Of those that a mesh axis runs over, the one named last changes fastest.
Arguments:
- normed: bfloat16 [16384, 4096], P(('dp', 'tensor')), may hold values from -24 to 24
- out_grad: bfloat16 [16384, 4096], P(('dp', 'tensor')), may hold values from -0.046875 to 0.046875
- attn_out: bfloat16 [16384, 4096], P('dp', 'tensor'), may hold values from -6 to 6
- d_query: bfloat16 [16384, 4096], P('dp', 'tensor'), may hold values from -0.046875 to 0.046875
- d_keyvalue: bfloat16 [16384, 4096], P('dp', 'tensor'), may hold values from -0.046875 to 0.046875
- positions: int32 [16384], P('dp'), may hold values from 0 to 4095
- w_query: bfloat16 [4096, 4096], P(None, 'tensor'), may hold values from -8 to 8
- w_keyvalue: bfloat16 [4096, 2048], P(None, 'tensor'), may hold values from -8 to 8
Outputs:
- hidden_grad: bfloat16 [16384, 4096], P(('dp', 'tensor'))
- query_weight_grad: bfloat16 [4096, 4096], P('dp', 'tensor')
- keyvalue_weight_grad: bfloat16 [4096, 2048], P('dp', 'tensor')
- out_weight_grad: bfloat16 [4096, 4096], P('tensor', 'dp')
All inputs are finite; a program needn't handle non-finite values.
Results may differ from a plain program's by a relative error of at most 0.023.
Values may be sent and summed in bfloat16 or wider, within the bound.
A program may use at most 128 MiB of HBM per device.

v0:
```python
import jax
import jax.numpy as jnp
from jax import lax
from jax.sharding import PartitionSpec as P


def from_partner(value, axis, distance):
    mask = 2**distance
    pairs = [(source, source ^ mask) for source in range(lax.axis_size(axis))]
    return lax.ppermute(value, axis, pairs)


def rotary_tables(positions, head_dim):
    half_width = head_dim // 2
    inverse = jnp.power(
        jnp.float32(1000000.0), -(jnp.arange(half_width, dtype=jnp.float32) * 2.0 / head_dim)
    )
    angles = positions.astype(jnp.float32)[:, None] * inverse[None, :]
    angles = jnp.concatenate([angles, angles], axis=1)
    return (jnp.cos(angles), jnp.sin(angles))


def rotary_back(grad_vals, cosine, sine):
    half_width = grad_vals.shape[-1] // 2
    scaled = grad_vals * sine
    turned = jnp.concatenate([scaled[..., half_width:], -scaled[..., :half_width]], axis=-1)
    return grad_vals * cosine + turned


def contract(left, right, left_dim, right_dim):
    return lax.dot_general(
        left, right, (((left_dim,), (right_dim,)), ((), ())), preferred_element_type=jnp.float32
    )


def local(normed, out_grad, attn_out, d_query, d_keyvalue, positions, w_query, w_keyvalue):
    tok_rows = d_query.shape[0]
    query_width = d_query.shape[1]
    head_dim = w_keyvalue.shape[1]
    cosine, sine = rotary_tables(positions, head_dim)
    cosine = cosine[:, None, :]
    sine = sine[:, None, :]
    query_grad = rotary_back(
        d_query.astype(jnp.float32).reshape(tok_rows, query_width // head_dim, head_dim),
        cosine,
        sine,
    )
    query_grad = query_grad.reshape(tok_rows, query_width).astype(jnp.bfloat16)
    pairs = d_keyvalue.astype(jnp.float32).reshape(tok_rows, 2, head_dim)
    key_part = rotary_back(pairs[:, 0:1, :], cosine, sine)[:, 0, :]
    keyvalue_grad = jnp.concatenate([key_part, pairs[:, 1, :]], axis=1).astype(jnp.bfloat16)
    parity = lax.axis_index("tensor") % 2
    own_half = lax.dynamic_slice_in_dim(keyvalue_grad, parity * head_dim, head_dim, 1)
    other_half = lax.dynamic_slice_in_dim(keyvalue_grad, (1 - parity) * head_dim, head_dim, 1)
    partner = from_partner(other_half, "tensor", 0)
    grad_rows = jnp.concatenate([query_grad, own_half, partner], axis=1)
    w_joined = jnp.concatenate([w_query, w_keyvalue, w_keyvalue], axis=1)
    selected = grad_rows
    hidden_grad = lax.psum_scatter(
        contract(selected, w_joined, 1, 1).astype(jnp.bfloat16),
        "tensor",
        scatter_dimension=0,
        tiled=True,
    )
    selected = attn_out
    out_total = contract(selected, lax.all_gather(out_grad, "tensor", axis=0, tiled=True), 0, 0)
    selected = grad_rows
    proj_total = contract(lax.all_gather(normed, "tensor", axis=0, tiled=True), selected, 0, 0)
    query_part = proj_total[:, :query_width]
    keyvalue_part = (
        proj_total[:, query_width : query_width + head_dim]
        + proj_total[:, query_width + head_dim :]
    )
    query_sum = lax.psum_scatter(
        query_part.astype(jnp.bfloat16), "dp", scatter_dimension=0, tiled=True
    )
    keyvalue_sum = lax.psum_scatter(
        keyvalue_part.astype(jnp.bfloat16), "dp", scatter_dimension=0, tiled=True
    )
    out_sum = lax.psum_scatter(
        out_total.astype(jnp.bfloat16), "dp", scatter_dimension=1, tiled=True
    )
    return (hidden_grad, query_sum, keyvalue_sum, out_sum)


def solution(mesh):
    return jax.shard_map(
        local,
        mesh=mesh,
        in_specs=(
            P(("dp", "tensor"), None),
            P(("dp", "tensor"), None),
            P("dp", "tensor"),
            P("dp", "tensor"),
            P("dp", "tensor"),
            P("dp"),
            P(None, "tensor"),
            P(None, "tensor"),
        ),
        out_specs=(
            P(("dp", "tensor"), None),
            P("dp", "tensor"),
            P("dp", "tensor"),
            P("tensor", "dp"),
        ),
        check_vma=False,
    )
```

profile of v0, /device:TPU:8, one launch (start us, length us, event | category | flops | bytes accessed | tf_op | source)
XLA Modules:
  0.0 838.1 jit_solution(3271912965196292895)
XLA Ops:
  7.2 0.0 copy-start
  7.2 0.0 all-gather.3.cloned.1.call-start
  7.2 0.7 all-gather.3.cloned.1.call-update
  7.9 0.0 all-gather.5.cloned.1.call-start
  8.0 0.7 all-gather.5.cloned.1.call-update
  8.7 0.0 reduce-scatter.9.cloned.1.call-start
  8.7 1.2 reshape.152
  9.9 0.7 convert_element_type.22
  10.6 0.7 fusion.18
  11.4 0.0 copy-start.2
  11.4 0.2 broadcast_multiply_fusion.1
  11.6 1.9 convert_multiply_fusion
  13.6 0.2 fusion.19
  13.8 2.0 fusion.13
  15.8 0.2 fusion.12
  16.0 0.1 collective-permute-start
  16.1 0.0 copy-done.2
  16.1 0.5 reshape.151
  16.7 2.2 fusion.10
  18.9 0.6 broadcast_multiply_fusion
  19.5 1.5 fusion.17
  21.0 1.1 pad_maximum_fusion
  22.1 0.4 mul.65
  22.5 0.3 fusion.6
  22.8 0.0 collective-permute-done
  22.8 44.6 %all-gather.3.cloned.1.call-done = bf16[1024,4096]{1,0:T(8,128)(2,1)} async-done(((bf16[64,4096]{1,0:T(8,128)(2,1)}), bf16[1024,4096]{1,0:T(8,128)(2,1)}) %all-gather.3.cloned.1.call-update) | async-done | bytes 8388624 | tf_op jit(solution)/shard_map/all_gather | solution.py:68
  67.4 7.1 convolution_bitcast_fusion
  74.6 0.0 copy-start.1
  74.6 3.2 copy-done.1
  77.8 1.2 fusion.5
  79.0 0.0 copy-start.3
  79.0 0.0 reduce-scatter.9.cloned.1.call-update
  79.0 0.2 reduce-scatter.7.cloned.1.call-start
  79.3 3.9 slice.66
  83.1 0.0 reduce-scatter.7.cloned.1.call-update
  83.2 0.0 reduce-scatter.5.cloned.1.call-start
  83.2 0.0 copy-done.3
  83.2 8.3 convolution_convert_fusion
  91.5 0.0 reduce-scatter.5.cloned.1.call-update
  91.6 0.0 reduce-scatter.11.cloned.1.call-start
  91.6 33.4 %all-gather.5.cloned.1.call-done = bf16[1024,4096]{1,0:T(8,128)(2,1)} async-done(((bf16[64,4096]{1,0:T(8,128)(2,1)}), bf16[1024,4096]{1,0:T(8,128)(2,1)}) %all-gather.5.cloned.1.call-update) | async-done | bytes 8388624 | tf_op jit(solution)/shard_map/all_gather | solution.py:66
  125.0 0.0 copy-done
  125.0 7.1 convolution_convert_fusion.1
  132.1 0.0 reduce-scatter.11.cloned.1.call-update
  132.1 200.6 %reduce-scatter.9.cloned.1.call-done = bf16[256,128]{0,1:T(8,128)(2,1)} async-done(((bf16[4096,128]{0,1:T(8,128)(2,1)}), bf16[256,128]{0,1:T(8,128)(2,1)}) %reduce-scatter.9.cloned.1.call-update) | async-done | bytes 65552 | tf_op jit(solution)/shard_map/reduce_scatter | solution.py:77
  332.7 1.6 copy.15
  334.2 208.1 %reduce-scatter.7.cloned.1.call-done = bf16[256,256]{0,1:T(8,128)(2,1)} async-done(((bf16[4096,256]{0,1:T(8,128)(2,1)}), bf16[256,256]{0,1:T(8,128)(2,1)}) %reduce-scatter.7.cloned.1.call-update) | async-done | bytes 131088 | tf_op jit(solution)/shard_map/reduce_scatter | solution.py:74
  542.3 1.7 copy.14
  544.0 72.0 %reduce-scatter.5.cloned.1.call-done = bf16[64,4096]{1,0:T(8,128)(2,1)} async-done(((bf16[1024,4096]{1,0:T(8,128)(2,1)}), bf16[64,4096]{1,0:T(8,128)(2,1)}) %reduce-scatter.5.cloned.1.call-update) | async-done | bytes 524304 | tf_op jit(solution)/shard_map/reduce_scatter | solution.py:59
  615.9 215.3 %reduce-scatter.11.cloned.1.call-done = bf16[256,256]{1,0:T(8,128)(2,1)} async-done(((bf16[256,4096]{1,0:T(8,128)(2,1)}), bf16[256,256]{1,0:T(8,128)(2,1)}) %reduce-scatter.11.cloned.1.call-update) | async-done | bytes 131088 | tf_op jit(solution)/shard_map/reduce_scatter | solution.py:80
  (2 shorter events, 0.0 us)
Async XLA Ops:
  7.2 117.8 %copy-start = (bf16[1024,256]{1,0:T(8,128)(2,1)S(1)}, bf16[1024,256]{1,0:T(8,128)(2,1)}, u32[]{:S(2)}) copy-start(bf16[1024,256]{1,0:T(8,128)(2,1)} %param.10) | copy-start | bytes 1572868
  7.2 60.3 %all-gather.3.cloned.1.call-start = ((), (), s32[]{:S(2)}) async-start(), calls=%async_computation.5 | async-start | bytes 8912896 | tf_op jit(solution)/shard_map/all_gather | solution.py:68
  7.9 117.1 %all-gather.5.cloned.1.call-start = ((), (), s32[]{:S(2)}) async-start(), calls=%async_computation.8 | async-start | bytes 8912896 | tf_op jit(solution)/shard_map/all_gather | solution.py:66
  8.7 324.0 %reduce-scatter.9.cloned.1.call-start = ((), (), s32[]{:S(2)}) async-start(), calls=%async_computation.7 | async-start | bytes 1114112 | tf_op jit(solution)/shard_map/reduce_scatter | solution.py:77
  11.4 4.8 copy-start.2
  16.0 6.8 collective-permute-start
  74.6 3.2 copy-start.1
  79.0 4.2 copy-start.3
  79.0 463.3 %reduce-scatter.7.cloned.1.call-start = ((), (), s32[]{:S(2)}) async-start(), calls=%async_computation.6 | async-start | bytes 2228224 | tf_op jit(solution)/shard_map/reduce_scatter | solution.py:74
  83.2 532.8 %reduce-scatter.5.cloned.1.call-start = ((), (), s32[]{:S(2)}) async-start(), calls=%async_computation.4 | async-start | bytes 8912896 | tf_op jit(solution)/shard_map/reduce_scatter | solution.py:59
  91.6 739.7 %reduce-scatter.11.cloned.1.call-start = ((), (), s32[]{:S(2)}) async-start(), calls=%async_computation.9 | async-start | bytes 2228224 | tf_op jit(solution)/shard_map/reduce_scatter | solution.py:80
Sparse Core Ops, SparseCore 0:
  9.9 57.5 all-gather.2
  69.3 55.6 all-gather.4
  128.8 203.8 reduce-scatter.8
  336.4 205.8 reduce-scatter.6
  545.3 70.6 reduce-scatter.4
  620.3 210.9 reduce-scatter.10
where the time goes:
time: 838 us
  waiting for transfers between devices  775 us (92%)
  matrix products  22.5 us (3%)
  between operations  14.3 us (2%)
  local copies, waits for them, and re-layouts  13.2 us (2%)
  other arithmetic  12.2 us (1%)
    reduce_scatter x1, waiting for transfers between devices, local(): lax.psum_scatter(out_total.astype(jnp.bfloat16), 'dp', scatter_dimension=...  215 us
    reduce_scatter x1, waiting for transfers between devices, local(): lax.psum_scatter(query_part.astype(jnp.bfloat16), 'dp', scatter_dimension...  208 us
    reduce_scatter x1, waiting for transfers between devices, local(): lax.psum_scatter(keyvalue_part.astype(jnp.bfloat16), 'dp', scatter_dimens...  201 us
    reduce_scatter x1, waiting for transfers between devices, local(): lax.psum_scatter(contract(selected, w_joined, 1, 1).astype(jnp.bfloat16),...  72 us
    all_gather x1, waiting for transfers between devices, local(): lax.all_gather(normed, 'tensor', axis=0, tiled=True)  44.6 us
    all_gather x1, waiting for transfers between devices, local(): lax.all_gather(out_grad, 'tensor', axis=0, tiled=True)  33.4 us
    dot_general x3, matrix products, contract(): lax.dot_general(left, right, (((left_dim,), (right_dim,)), ((), ())), pre...  22.5 us
  transfers between devices with their start and end apart: 7, of which 6 were waited for; matrix products, arithmetic and copies ran while one was open for 5% of the time, Pallas kernels for 0%

commit v1 on v0

v1 whole, which is shorter than its diff:
```python
import functools

import jax
import jax.numpy as jnp
from jax import lax
from jax.experimental import pallas as pl
from jax.experimental.pallas import tpu as pltpu
from jax.sharding import PartitionSpec as P

MESH = pl.DeviceIdType.MESH
BF16 = jnp.bfloat16
F32 = jnp.float32

D = 4096
HD = 128
QW = 256
ROWS = QW + HD
TOK = 64
REP = 1024
BLK = 256
NZ = 8
NY = 4
AG_A = 2304
AG_B = D - AG_A
AG_B1 = 896
HR_A = 2304
HR_B = D - HR_A
HR_B1 = 896
SEMS = 112


def kernel(
    normed, out_grad, attn_out, d_query, d_keyvalue, cosine, sine, w_query, w_keyvalue,
    hidden_out, query_out, keyvalue_out, out_out,
    g_norm, g_out, w_cat, grads, h_grads, grads_t, attn_v, attn_t, q_in, kv_own, kv_other,
    cos_v, sin_v, part_h, rx_b, r2_a, r2_b1, r2_b2, ry_a, ry_b, rx_a, hs_a,
    ct_q, sb_q, rb_q, xs_q, xr_q, ct_o, sb_o, rb_o, xs_o, xr_o,
    send_sems, recv_sems, local_sems,
):
    dp = lax.axis_index("dp")
    tensor = lax.axis_index("tensor")
    c = tensor % 2
    y = (tensor // 2) % NY
    x = tensor // (2 * NY)
    z = dp % NZ
    h = dp // NZ
    xp = 1 - x
    yp, ym, y2 = (y + 1) % NY, (y + 3) % NY, (y + 2) % NY

    def tid(x_, y_, c_):
        return (x_ * NY + y_) * 2 + c_

    dev_x = (dp, tid(xp, y, c))
    dev_yp = (dp, tid(x, yp, c))
    dev_ym = (dp, tid(x, ym, c))
    dev_c = (dp, tid(x, y, 1 - c))
    dev_zp = (h * NZ + (z + 1) % NZ, tensor)
    dev_zm = (h * NZ + (z + NZ - 1) % NZ, tensor)
    dev_h = ((1 - h) * NZ + z, tensor)
    partners = (dev_x, dev_yp, dev_ym, dev_c, dev_zp, dev_zm, dev_h)

    messages = []
    locals_ = []

    def send(src, dst, device):
        at = len(messages)
        copy = pltpu.make_async_remote_copy(
            src_ref=src, dst_ref=dst, send_sem=send_sems.at[at], recv_sem=recv_sems.at[at],
            device_id=device, device_id_type=MESH,
        )
        copy.start()
        messages.append(copy)
        return copy

    def load(src, dst):
        copy = pltpu.make_async_copy(src, dst, local_sems.at[len(locals_)])
        copy.start()
        locals_.append(copy)
        return copy

    def gather(src, g):
        m = {}
        ca, cb = pl.ds(0, AG_A), pl.ds(AG_A, AG_B)
        cb1, cb2 = pl.ds(AG_A, AG_B1), pl.ds(AG_A + AG_B1, AG_B - AG_B1)
        full = pl.ds(0, D)

        def at(x_, y_, cols):
            return g.at[pl.ds(pl.multiple_of(tid(x_, y_, c) * TOK, TOK), TOK), cols]

        def go(name, x_, y_, cols, device):
            m[name] = send(at(x_, y_, cols), at(x_, y_, cols), device)

        def arrive(*names):
            for name in names:
                m[name].wait_recv()

        def s0():
            m["X0"] = send(src.at[:, ca], at(x, y, ca), dev_x)
            m["P0"] = send(src.at[:, cb], at(x, y, cb), dev_yp)
            m["M0"] = send(src.at[:, cb], at(x, y, cb), dev_ym)
            m["X1"] = send(src.at[:, cb], at(x, y, cb), dev_x)
            m["P1"] = send(src.at[:, ca], at(x, y, ca), dev_yp)
            m["M1"] = send(src.at[:, ca], at(x, y, ca), dev_ym)
            m["C0"] = send(src, at(x, y, full), dev_c)
            m["L"] = load(src, at(x, y, full))

        def s1():
            arrive("P0", "M0")
            go("P2", x, ym, cb1, dev_yp)
            go("M2", x, yp, cb2, dev_ym)
            go("X2", x, yp, cb, dev_x)
            go("X3", x, ym, cb, dev_x)

        def s2():
            arrive("X0")
            go("P3", xp, y, ca, dev_yp)
            go("M3", xp, y, ca, dev_ym)

        def s3():
            arrive("P1", "M1")
            go("P4", x, ym, ca, dev_yp)
            go("C1", x, ym, full, dev_c)
            go("C2", x, yp, full, dev_c)

        def s4():
            arrive("X1")
            go("C3", xp, y, full, dev_c)

        def s5():
            arrive("P2", "M2")
            go("X4", x, y2, cb, dev_x)

        def s6():
            arrive("P3", "M3")
            go("M4", xp, yp, ca, dev_ym)

        def s7():
            arrive("X2", "X3")
            go("C6", xp, yp, full, dev_c)
            go("C5", xp, ym, full, dev_c)

        def s8():
            arrive("P4")
            go("C4", x, y2, full, dev_c)
            arrive("M4", "X4")
            go("C7", xp, y2, full, dev_c)

        def s9():
            m["L"].wait()
            arrive(*("C%d" % i for i in range(8)))

        return s0, s1, s2, s3, s4, s5, s6, s7, s8, s9

    def reduce_dp(lhs, g, ct, sb, rb, xs, xr):
        m = {}

        def part(k, hh):
            cols = pl.ds(pl.multiple_of((hh * NZ + (z + k) % NZ) * BLK, BLK), BLK)
            return jnp.dot(lhs[...], g[:, cols], preferred_element_type=F32).astype(BF16)

        def slot(k):
            return 3 - k

        def s1():
            sb[0] = part(4, 0)
            m["P1"] = send(sb.at[0], rb.at[0, 0, 0], dev_zp)
            sb[1] = part(4, 1)
            m["M1"] = send(sb.at[1], rb.at[1, 0, 1], dev_zm)

            def body(i, carry):
                j = i // 2
                hh = i % 2
                ct[j, hh] = part(NZ + 3 - j, hh)
                return carry

            lax.fori_loop(0, 14, body, 0)

        def add(dst, value):
            return (dst.astype(F32) + value.astype(F32)).astype(BF16)

        def s2():
            m["P1"].wait_recv()
            rb[0, 0, 0] = add(rb[0, 0, 0], ct[slot(3), 0])
            rb[0, 0, 1] = ct[slot(3), 1]
            m["P2"] = send(rb.at[0, 0], rb.at[0, 1], dev_zp)
            m["M1"].wait_recv()
            rb[1, 0, 1] = add(rb[1, 0, 1], ct[slot(-3), 1])
            rb[1, 0, 0] = ct[slot(-3), 0]
            m["M2"] = send(rb.at[1, 0], rb.at[1, 1], dev_zm)

        def mid(s):
            k = 5 - s
            m["P%d" % (s - 1)].wait_recv()
            for hh in range(2):
                rb[0, s - 2, hh] = add(rb[0, s - 2, hh], ct[slot(k), hh])
            m["P%d" % s] = send(rb.at[0, s - 2], rb.at[0, s - 1], dev_zp)
            m["M%d" % (s - 1)].wait_recv()
            for hh in range(2):
                rb[1, s - 2, hh] = add(rb[1, s - 2, hh], ct[slot(-k), hh])
            m["M%d" % s] = send(rb.at[1, s - 2], rb.at[1, s - 1], dev_zm)

        def total(hh):
            return ct[slot(0), hh].astype(F32) + rb[0, 3, hh].astype(F32) + rb[1, 3, hh].astype(F32)

        def s5():
            m["P4"].wait_recv()
            m["M4"].wait_recv()
            xs[...] = total(1 - h).astype(BF16)
            m["H"] = send(xs, xr, dev_h)

        def s6():
            m["H"].wait_recv()
            return total(h) + xr[...].astype(F32)

        return s1, s2, functools.partial(mid, 3), functools.partial(mid, 4), s5, s6

    def reduce_hidden():
        m = {}
        ca, cb = pl.ds(0, HR_A), pl.ds(HR_A, HR_B)
        cb1, cb2 = pl.ds(HR_A, HR_B1), pl.ds(HR_A + HR_B1, HR_B - HR_B1)
        p = part_h

        def at(x_, y_):
            return x_ * NY + y_

        def add(d, cols, value):
            p[d, :, cols] = (p[d, :, cols].astype(F32) + value.astype(F32)).astype(BF16)

        def s0():
            m["HX0"] = send(p.at[pl.ds(xp * NY, NY), :, cb], rx_b, dev_x)
            m["HP0"] = send(p.at[at(x, y2), :, ca], r2_a.at[0], dev_yp)
            m["HM0"] = send(p.at[at(xp, y2), :, ca], r2_a.at[1], dev_ym)
            m["HP2b"] = send(p.at[at(xp, yp), :, ca], ry_a.at[0, 1], dev_yp)
            m["HM2a"] = send(p.at[at(x, ym), :, ca], ry_a.at[1, 0], dev_ym)

        def s1():
            m["HP0"].wait_recv()
            add(at(x, yp), ca, r2_a[0])
            m["HP2a"] = send(p.at[at(x, yp), :, ca], ry_a.at[0, 0], dev_yp)
            m["HM0"].wait_recv()
            add(at(xp, ym), ca, r2_a[1])
            m["HM2b"] = send(p.at[at(xp, ym), :, ca], ry_a.at[1, 1], dev_ym)

        def s2():
            m["HX0"].wait_recv()
            add(at(x, y2), cb, rx_b[y2])
            m["HP1"] = send(p.at[at(x, y2), :, cb1], r2_b1, dev_yp)
            m["HM1"] = send(p.at[at(x, y2), :, cb2], r2_b2, dev_ym)
            for y_ in (yp, ym, y):
                add(at(x, y_), cb, rx_b[y_])

        def s3():
            m["HP1"].wait_recv()
            add(at(x, yp), cb1, r2_b1[...])
            m["HP3"] = send(p.at[at(x, yp), :, cb], ry_b.at[0], dev_yp)
            m["HM1"].wait_recv()
            add(at(x, ym), cb2, r2_b2[...])
            m["HM3"] = send(p.at[at(x, ym), :, cb], ry_b.at[1], dev_ym)

        def s4():
            m["HP2b"].wait_recv()
            m["HM2b"].wait_recv()
            d = at(xp, y)
            hs_a[...] = (
                p[d, :, ca].astype(F32) + ry_a[0, 1].astype(F32) + ry_a[1, 1].astype(F32)
            ).astype(BF16)
            m["HX1"] = send(hs_a, rx_a, dev_x)

        def s5():
            for name in ("HP2a", "HM2a", "HP3", "HM3", "HX1"):
                m[name].wait_recv()
            d = at(x, y)
            hidden_out[:, ca] = (
                (p[d, :, ca].astype(F32) + ry_a[0, 0].astype(F32))
                + (ry_a[1, 0].astype(F32) + rx_a[...].astype(F32))
            ).astype(BF16)
            hidden_out[:, cb] = (
                p[d, :, cb].astype(F32) + ry_b[0].astype(F32) + ry_b[1].astype(F32)
            ).astype(BF16)

        return s0, s1, s2, s3, s4, s5

    def rotate_all():
        key = (1 - c).astype(F32)

        def body(d, carry):
            rows = pl.ds(pl.multiple_of(d * 2 * TOK, 2 * TOK), 2 * TOK)
            cs, sn = cos_v[rows, :], sin_v[rows, :]
            for head in range(QW // HD):
                cols = pl.ds(head * HD, HD)
                g = q_in[rows, cols].astype(F32)
                turned = g * cs + pltpu.roll(g, HD // 2, 1) * sn
                grads[d, :, :, cols] = turned.astype(BF16).reshape(2, TOK, HD)
            g = kv_own[rows, :].astype(F32) + kv_other[rows, :].astype(F32)
            cs, sn = cs * key + (1.0 - key), sn * key
            turned = g * cs + pltpu.roll(g, HD // 2, 1) * sn
            grads[d, :, :, pl.ds(QW, HD)] = turned.astype(BF16).reshape(2, TOK, HD)
            return carry

        lax.fori_loop(0, REP // (2 * TOK), body, 0)

    def transpose_all():
        def body(d, carry):
            cols = pl.ds(pl.multiple_of(d * 2 * TOK, 2 * TOK), 2 * TOK)
            grads_t[:, cols] = grads[d].reshape(2 * TOK, ROWS).T
            attn_t[:, cols] = attn_v[cols, :].T
            return carry

        lax.fori_loop(0, REP // (2 * TOK), body, 0)

    def hidden_partials():
        step = 512

        def body(i, carry):
            cols = pl.ds(pl.multiple_of(i * step, step), step)
            total = lax.dot_general(
                h_grads[...].reshape(REP // 2, 2 * ROWS), w_cat[cols, :],
                (((1,), (1,)), ((), ())), preferred_element_type=F32,
            )
            part_h[:, :, cols] = total.astype(BF16).reshape(2 * NY, TOK, step)
            return carry

        lax.fori_loop(0, D // step, body, 0)

    barrier = pltpu.get_barrier_semaphore()
    for device in partners:
        pl.semaphore_signal(barrier, inc=1, device_id=device, device_id_type=MESH)
    l_cos = load(cosine, cos_v)
    l_sin = load(sine, sin_v)
    l_q = load(d_query, q_in)
    l_kv = load(d_keyvalue.at[:, pl.ds(pl.multiple_of(c * HD, HD), HD)], kv_own)
    l_attn = load(attn_out, attn_v)
    l_wq = load(w_query, w_cat.at[:, pl.ds(0, QW)])
    l_wkv = load(w_keyvalue, w_cat.at[:, pl.ds(QW, HD)])
    pl.semaphore_wait(barrier, len(partners))

    a1 = gather(normed, g_norm)
    a2 = gather(out_grad, g_out)
    r1 = reduce_dp(grads_t, g_norm, ct_q, sb_q, rb_q, xs_q, xr_q)
    r2 = reduce_dp(attn_t, g_out, ct_o, sb_o, rb_o, xs_o, xr_o)
    hr = reduce_hidden()

    k_kv = send(
        d_keyvalue.at[:, pl.ds(pl.multiple_of((1 - c) * HD, HD), HD)], kv_other, dev_c
    )
    a1[0]()
    k_wq = send(w_query, w_cat.at[:, pl.ds(ROWS, QW)], dev_c)
    k_wkv = send(w_keyvalue, w_cat.at[:, pl.ds(ROWS + QW, HD)], dev_c)
    for copy in (l_cos, l_sin, l_q, l_kv):
        copy.wait()
    k_kv.wait_recv()
    rotate_all()
    k_g = send(grads.at[:, 1 - c], h_grads.at[:, :, pl.ds(ROWS, ROWS)], dev_c)
    l_g = load(grads.at[:, c], h_grads.at[:, :, pl.ds(0, ROWS)])
    a1[1]()
    a1[2]()
    l_attn.wait()
    transpose_all()
    a1[3]()
    a1[4]()
    a1[5]()
    a1[6]()
    a2[0]()
    for copy in (l_wq, l_wkv, l_g):
        copy.wait()
    for copy in (k_wq, k_wkv, k_g):
        copy.wait_recv()
    hidden_partials()
    a1[7]()
    a1[8]()
    a1[9]()
    r1[0]()
    a2[1]()
    a2[2]()
    r1[1]()
    a2[3]()
    a2[4]()
    a2[5]()
    r1[2]()
    a2[6]()
    hr[0]()
    a2[7]()
    a2[8]()
    a2[9]()
    r2[0]()
    r1[3]()
    hr[1]()
    r2[1]()
    hr[2]()
    r1[4]()
    r2[2]()
    hr[3]()
    total = r1[5]()
    query_out[...] = total[:QW].T.astype(BF16)
    keyvalue_out[...] = total[QW:].T.astype(BF16)
    hr[4]()
    r2[3]()
    r2[4]()
    hr[5]()
    out_out[...] = r2[5]().astype(BF16)
    for message in messages:
        message.wait_send()


def rotary_tables(positions):
    half = HD // 2
    inverse = jnp.power(F32(1000000.0), -(jnp.arange(half, dtype=F32) * 2.0 / HD))
    angles = positions.astype(F32)[:, None] * inverse[None, :]
    cosine, sine = jnp.cos(angles), jnp.sin(angles)
    return jnp.concatenate([cosine, cosine], axis=1), jnp.concatenate([sine, -sine], axis=1)


def local(normed, out_grad, attn_out, d_query, d_keyvalue, positions, w_query, w_keyvalue):
    cosine, sine = rotary_tables(positions)
    vmem = pltpu.VMEM
    return pl.pallas_call(
        kernel,
        out_shape=(
            jax.ShapeDtypeStruct((TOK, D), BF16),
            jax.ShapeDtypeStruct((BLK, QW), BF16),
            jax.ShapeDtypeStruct((BLK, HD), BF16),
            jax.ShapeDtypeStruct((QW, BLK), BF16),
        ),
        in_specs=[pl.BlockSpec(memory_space=pl.ANY)] * 9,
        out_specs=[pl.BlockSpec(memory_space=vmem)] * 4,
        scratch_shapes=[
            vmem((REP, D), BF16),
            vmem((REP, D), BF16),
            vmem((D, 2 * ROWS), BF16),
            vmem((2 * NY, 2, TOK, ROWS), BF16),
            vmem((2 * NY, TOK, 2 * ROWS), BF16),
            vmem((ROWS, REP), BF16),
            vmem((REP, QW), BF16),
            vmem((QW, REP), BF16),
            vmem((REP, QW), BF16),
            vmem((REP, HD), BF16),
            vmem((REP, HD), BF16),
            vmem((REP, HD), F32),
            vmem((REP, HD), F32),
            vmem((2 * NY, TOK, D), BF16),
            vmem((NY, TOK, HR_B), BF16),
            vmem((2, TOK, HR_A), BF16),
            vmem((TOK, HR_B1), BF16),
            vmem((TOK, HR_B - HR_B1), BF16),
            vmem((2, 2, TOK, HR_A), BF16),
            vmem((2, TOK, HR_B), BF16),
            vmem((TOK, HR_A), BF16),
            vmem((TOK, HR_A), BF16),
        ]
        + [
            shape
            for rows in (ROWS, QW)
            for shape in (
                vmem((7, 2, rows, BLK), BF16),
                vmem((2, rows, BLK), BF16),
                vmem((2, 4, 2, rows, BLK), BF16),
                vmem((rows, BLK), BF16),
                vmem((rows, BLK), BF16),
            )
        ]
        + [
            pltpu.SemaphoreType.DMA((SEMS,)),
            pltpu.SemaphoreType.DMA((SEMS,)),
            pltpu.SemaphoreType.DMA((16,)),
        ],
        compiler_params=pltpu.CompilerParams(
            collective_id=0, has_side_effects=True, vmem_limit_bytes=60 * 1024 * 1024
        ),
    )(normed, out_grad, attn_out, d_query, d_keyvalue, cosine, sine, w_query, w_keyvalue)


def solution(mesh):
    return jax.shard_map(
        local,
        mesh=mesh,
        in_specs=(
            P(("dp", "tensor"), None),
            P(("dp", "tensor"), None),
            P("dp", "tensor"),
            P("dp", "tensor"),
            P("dp", "tensor"),
            P("dp"),
            P(None, "tensor"),
            P(None, "tensor"),
        ),
        out_specs=(
            P(("dp", "tensor"), None),
            P("dp", "tensor"),
            P("dp", "tensor"),
            P("tensor", "dp"),
        ),
        check_vma=False,
    )
```

time: 838 us -> 124 us (0.15)
  the two profiles are of different devices: /device:TPU:8 before, /device:TPU:48 now
where the time goes in v1:
time: 124 us
  Pallas kernels  113 us (91%)
  local copies, waits for them, and re-layouts  6.47 us (5%)
  other arithmetic  3.91 us (3%)
    pallas_call x1, Pallas kernels, local(): pl.pallas_call(kernel, out_shape=(jax.ShapeDtypeStruct((TOK, D), BF16), j...  113 us
    unnamed x4, local copies, waits for them, and re-layouts  6.47 us

profile of v1, /device:TPU:48, one launch (start us, length us, event | category | flops | bytes accessed | tf_op | source)
XLA Modules:
  0.0 124.1 jit_solution(10321521350901723874)
XLA Ops:
  0.6 0.7 convert_element_type.3
  1.3 1.9 %multiply_sine_fusion = (f32[1024,64]{1,0:T(8,128)S(1)}, f32[1024,64]{1,0:T(8,128)S(1)}, f32[1024,64]{1,0:T(8,128)S(1)}) fusion(f32[64]{0:T(128)S(1)} %negate_power_fusion, f32[1024]{0:T(1024)S(1)} %convert_element_type.3), kind=kLoop, calls=%fused_computation | loop fusion | flops 131072 | bytes 790784 | tf_op jit(solution)/shard_map/sin | solution.py:409
  3.2 1.3 %pad_maximum_fusion = (f32[1024,128]{1,0:T(8,128)}, f32[1024,128]{1,0:T(8,128)}) fusion(f32[1024,64]{1,0:T(8,128)S(1)} %get-tuple-element.6, f32[1024,64]{1,0:T(8,128)S(1)} %get-tuple-element.5, f32[1024,64]{1,0:T(8,128)S(1)} %get-tuple-element.4), kind=kLoop, calls=%fused_computation.2 | loop fusion | flops 262144 | bytes 1835008 | tf_op jit(solution)/shard_map/concatenate | solution.py:410
  4.6 113.0 %shard_map.111 = (bf16[64,4096]{1,0:T(8,128)(2,1)}, bf16[256,256]{1,0:T(8,128)(2,1)}, bf16[256,128]{1,0:T(8,128)(2,1)}, bf16[256,256]{1,0:T(8,128)(2,1)}) custom-call(bf16[64,4096]{1,0:T(8,128)(2,1)} %normed.1, bf16[64,4096]{1,0:T(8,128)(2,1)} %out_grad.1, bf16[1024,256]{1,0:T(8,128)(2,1)} %attn_out.1, bf16[1024,256]{1,0:T(8,128)(2,1)} %d_query.1, ...), custom_call_target="tpu_custom_call" | custom-call | tf_op jit(solution)/shard_map/pallas_call | solution.py:416
  117.6 1.9 %copy.16 = bf16[64,4096]{1,0:T(8,128)(2,1)} copy(bf16[64,4096]{1,0:T(8,128)(2,1)} %get-tuple-element.13) | data formatting | bytes 1048576
  119.5 1.6 %copy.17 = bf16[256,256]{1,0:T(8,128)(2,1)} copy(bf16[256,256]{1,0:T(8,128)(2,1)} %get-tuple-element.14) | data formatting | bytes 262144
  121.0 1.5 %copy.18 = bf16[256,128]{1,0:T(8,128)(2,1)} copy(bf16[256,128]{1,0:T(8,128)(2,1)} %get-tuple-element.15) | data formatting | bytes 131072
  122.5 1.6 %copy.19 = bf16[256,256]{1,0:T(8,128)(2,1)} copy(bf16[256,256]{1,0:T(8,128)(2,1)} %get-tuple-element.16) | data formatting | bytes 262144
  (1 shorter events, 0.0 us)

commit v2 on v1

v2 whole, which is shorter than its diff:
```python
import functools

import jax
import jax.numpy as jnp
from jax import lax
from jax.experimental import pallas as pl
from jax.experimental.pallas import tpu as pltpu
from jax.sharding import PartitionSpec as P

MESH = pl.DeviceIdType.MESH
BF16 = jnp.bfloat16
F32 = jnp.float32

D = 4096
HD = 128
QW = 256
ROWS = QW + HD
TOK = 64
REP = 1024
LOG_BASE = 13.815510557964274
BLK = 256
NZ = 8
NY = 4
ORDER = (4, 3, -3, 2, -2, 1, -1, 0)
SLOTS = 2 * NZ
PHASES = {1: ((0, 5, 3), (8, 4, 4)), 2: ((0, 4, 4), (8, 5, 3))}
HR_A = 2816
HR_B = D - HR_A
HR_B1 = 640
SEMS = 160
LOCAL_SEMS = 48

PLAN = (
    99, 0, 1, 100, 101, 2, 102, 3, 5, 4, 6, 12, 7, 8, 13, 103, 9, 104, 10, 105, 106, 14, 15, 17,
    11, 48, 16, 49, 18, 24, 57, 50, 58, 51, 19, 25, 20, 21, 56, 59, 22, 23, 26, 27, 61, 52, 62,
    53, 28, 29, 54, 30, 36, 60, 63, 55, 31, 37, 65, 33, 32, 66, 34, 38, 64, 67, 35, 69, 70, 39,
    78, 40, 71, 42, 41, 90, 79, 72, 43, 91, 68, 44, 45, 77, 46, 80, 47, 73, 82, 92, 83, 74, 75,
    76, 81, 84, 94, 93, 86, 87, 96, 85, 88, 89, 95, 97, 107, 108, 98,
)


def kernel(
    normed, out_grad, attn_out, d_query, d_keyvalue, positions, w_query, w_keyvalue,
    hidden_out, query_out, keyvalue_out, out_out,
    g_norm, g_out, w_cat, grads, h_grads, grads_t, attn_v, attn_t, q_in, kv_own, kv_other,
    pos_v, part_h, rx_b, r2_a, r2_b1, r2_b2, ry_a, ry_b, rx_a, hs_a,
    ct_q, sb_q, rb_q, xs_q, xr_q, ct_o, sb_o, rb_o, xs_o, xr_o,
    send_sems, recv_sems, local_sems,
):
    dp = lax.axis_index("dp")
    tensor = lax.axis_index("tensor")
    c = tensor % 2
    y = (tensor // 2) % NY
    x = tensor // (2 * NY)
    z = dp % NZ
    h = dp // NZ
    xp = 1 - x
    yp, ym, y2 = (y + 1) % NY, (y + 3) % NY, (y + 2) % NY

    def tid(x_, y_, c_):
        return (x_ * NY + y_) * 2 + c_

    dev_x = (dp, tid(xp, y, c))
    dev_yp = (dp, tid(x, yp, c))
    dev_ym = (dp, tid(x, ym, c))
    dev_c = (dp, tid(x, y, 1 - c))
    dev_zp = (h * NZ + (z + 1) % NZ, tensor)
    dev_zm = (h * NZ + (z + NZ - 1) % NZ, tensor)
    dev_h = ((1 - h) * NZ + z, tensor)
    partners = (dev_x, dev_yp, dev_ym, dev_c, dev_zp, dev_zm, dev_h)

    messages = []
    locals_ = []

    def send(src, dst, device):
        at = len(messages)
        copy = pltpu.make_async_remote_copy(
            src_ref=src, dst_ref=dst, send_sem=send_sems.at[at], recv_sem=recv_sems.at[at],
            device_id=device, device_id_type=MESH,
        )
        copy.start()
        messages.append(copy)
        return copy

    def load(src, dst):
        copy = pltpu.make_async_copy(src, dst, local_sems.at[len(locals_)])
        copy.start()
        locals_.append(copy)
        return copy

    def columns(j, hh):
        return pl.ds(pl.multiple_of((hh * NZ + (z + NZ + ORDER[j]) % NZ) * BLK, BLK), BLK)

    def load_own(src, g):
        rows = pl.ds(pl.multiple_of(tensor * TOK, TOK), TOK)
        return [
            load(src.at[:, columns(i // 2, i % 2)], g.at[i, rows, :]) for i in range(SLOTS)
        ]

    def gather(g, own, phase, steps):
        first, count_a, count_b = phase
        m = {}
        ca, cb = pl.ds(first, count_a), pl.ds(first + count_a, count_b)
        full = pl.ds(first, count_a + count_b)

        def go(name, x_, y_, slots, device, part=None):
            row = tid(x_, y_, c) * TOK
            size = TOK if part is None else TOK // 2
            row = pl.multiple_of(row + (size if part else 0), TOK // 2)
            ref = g.at[slots, pl.ds(row, size), :]
            m[name] = send(ref, ref, device)

        def arrive(*names):
            for name in names:
                m[name].wait_recv()

        def ownx():
            for copy in own[first:first + count_a + count_b]:
                copy.wait()
            go("X0", x, y, ca, dev_x)
            go("X1", x, y, cb, dev_x)

        def own_y():
            go("P0", x, y, cb, dev_yp)
            go("M0", x, y, cb, dev_ym)
            go("P1", x, y, ca, dev_yp)
            go("M1", x, y, ca, dev_ym)
            go("C0", x, y, full, dev_c)

        def p0():
            arrive("P0", "M0")
            go("P2", x, ym, cb, dev_yp, 0)
            go("M2", x, yp, cb, dev_ym, 1)
            go("X3", x, ym, cb, dev_x)
            go("X2", x, yp, cb, dev_x)

        def x0():
            arrive("X0")
            go("P3", xp, y, ca, dev_yp)
            go("M3", xp, y, ca, dev_ym)

        def p1():
            arrive("P1", "M1")
            go("P4", x, ym, ca, dev_yp, 0)
            go("M4", x, yp, ca, dev_ym, 1)
            go("C1", x, ym, full, dev_c)
            go("C2", x, yp, full, dev_c)

        def x1():
            arrive("X1")
            go("C3", xp, y, full, dev_c)

        def p2():
            arrive("P2", "M2")
            go("X4", x, y2, cb, dev_x, 0)
            go("X5", x, y2, cb, dev_x, 1)

        def p3():
            arrive("P3", "M3")
            go("P5", xp, ym, ca, dev_yp, 0)
            go("M5", xp, yp, ca, dev_ym, 1)

        def c6():
            arrive("X2", "X3")
            go("C6", xp, yp, full, dev_c)
            go("C5", xp, ym, full, dev_c)

        def c4():
            arrive("P4", "M4")
            go("C4", x, y2, full, dev_c)

        def c7():
            arrive("P5", "M5", "X4", "X5")
            go("C7", xp, y2, full, dev_c)

        def done():
            arrive(*("C%d" % i for i in range(8)))

        steps.extend((ownx, own_y, p0, x0, p1, x1, p2, p3, c6, c4, c7, done))

    def reduce_dp(lhs, g, ct, sb, rb, xs, xr, steps):
        m = {}

        def product(i):
            return jnp.dot(lhs[...], g[i], preferred_element_type=F32).astype(BF16)

        def first():
            sb[0] = product(0)
            m["P1", 0] = send(sb.at[0], rb.at[0, 0, 0], dev_zp)
            sb[1] = product(1)
            m["M1", 1] = send(sb.at[1], rb.at[1, 0, 1], dev_zm)

        def part(j):
            def body(hh, carry):
                ct[j - 1, hh] = product(2 * j + hh)
                return carry

            lax.fori_loop(0, 2, body, 0)

        def slot(k):
            return ORDER.index(k) - 1

        def forward(side, s, hh):
            k = 5 - s if side == "P" else s - 5
            d = 0 if side == "P" else 1
            if s == 2 and hh != d:
                source = ct.at[slot(k), hh]
            else:
                m[side + str(s - 1), hh].wait_recv()
                source = rb.at[d, s - 2, hh]
                source[...] = (source[...].astype(F32) + ct[slot(k), hh].astype(F32)).astype(BF16)
            m[side + str(s), hh] = send(
                source, rb.at[d, s - 1, hh], dev_zp if side == "P" else dev_zm
            )

        def total(hh):
            return ct[slot(0), hh].astype(F32) + rb[0, 3, hh].astype(F32) + rb[1, 3, hh].astype(F32)

        def exchange():
            for hh in range(2):
                m["P4", hh].wait_recv()
                m["M4", hh].wait_recv()
            xs[...] = total(1 - h).astype(BF16)
            m["H"] = send(xs, xr, dev_h)

        def finish():
            m["H"].wait_recv()
            return total(h) + xr[...].astype(F32)

        steps.append(first)
        steps.extend(functools.partial(part, j) for j in range(1, NZ))
        steps.extend(
            functools.partial(forward, side, s, hh)
            for s in (2, 3, 4) for side in "PM" for hh in range(2)
        )
        steps.append(exchange)
        return finish

    def reduce_hidden(steps):
        m = {}
        ca, cb = pl.ds(0, HR_A), pl.ds(HR_A, HR_B)
        cb1, cb2 = pl.ds(HR_A, HR_B1), pl.ds(HR_A + HR_B1, HR_B - HR_B1)
        p = part_h

        def at(x_, y_):
            return x_ * NY + y_

        def add(d, cols, value):
            p[d, :, cols] = (p[d, :, cols].astype(F32) + value.astype(F32)).astype(BF16)

        def hr0x():
            for i, y_ in enumerate((y2, yp, ym, y)):
                m["HX0", i] = send(p.at[at(xp, y_), :, cb], rx_b.at[i], dev_x)

        def hr0():
            m["HP0"] = send(p.at[at(x, y2), :, ca], r2_a.at[0], dev_yp)
            m["HM0"] = send(p.at[at(xp, y2), :, ca], r2_a.at[1], dev_ym)
            m["HP2b"] = send(p.at[at(xp, yp), :, ca], ry_a.at[0, 1], dev_yp)

        def hr1():
            m["HX0", 0].wait_recv()
            add(at(x, y2), cb, rx_b[0])
            m["HP1"] = send(p.at[at(x, y2), :, cb1], r2_b1, dev_yp)
            m["HM1"] = send(p.at[at(x, y2), :, cb2], r2_b2, dev_ym)

        def hr2m():
            m["HM0"].wait_recv()
            add(at(xp, ym), ca, r2_a[1])
            m["HM2b"] = send(p.at[at(xp, ym), :, ca], ry_a.at[1, 1], dev_ym)
            m["HM2a"] = send(p.at[at(x, ym), :, ca], ry_a.at[1, 0], dev_ym)

        def hr2p():
            m["HP0"].wait_recv()
            add(at(x, yp), ca, r2_a[0])
            m["HP2a"] = send(p.at[at(x, yp), :, ca], ry_a.at[0, 0], dev_yp)

        def hr3p():
            m["HX0", 1].wait_recv()
            add(at(x, yp), cb, rx_b[1])
            m["HP1"].wait_recv()
            add(at(x, yp), cb1, r2_b1[...])
            m["HP3"] = send(p.at[at(x, yp), :, cb], ry_b.at[0], dev_yp)

        def hr3m():
            m["HX0", 2].wait_recv()
            add(at(x, ym), cb, rx_b[2])
            m["HM1"].wait_recv()
            add(at(x, ym), cb2, r2_b2[...])
            m["HM3"] = send(p.at[at(x, ym), :, cb], ry_b.at[1], dev_ym)

        def hr4():
            m["HP2b"].wait_recv()
            m["HM2b"].wait_recv()
            d = at(xp, y)
            hs_a[...] = (
                p[d, :, ca].astype(F32) + ry_a[0, 1].astype(F32) + ry_a[1, 1].astype(F32)
            ).astype(BF16)
            m["HX1"] = send(hs_a, rx_a, dev_x)

        def hr5():
            d = at(x, y)
            m["HX0", 3].wait_recv()
            for name in ("HP2a", "HM2a", "HP3", "HM3", "HX1"):
                m[name].wait_recv()
            hidden_out[:, ca] = (
                (p[d, :, ca].astype(F32) + ry_a[0, 0].astype(F32))
                + (ry_a[1, 0].astype(F32) + rx_a[...].astype(F32))
            ).astype(BF16)
            hidden_out[:, cb] = (
                (p[d, :, cb].astype(F32) + rx_b[3].astype(F32))
                + (ry_b[0].astype(F32) + ry_b[1].astype(F32))
            ).astype(BF16)

        steps.extend((hr0x, hr0, hr1, hr2m, hr2p, hr3p, hr3m, hr4, hr5))

    def rotate_all():
        key = (1 - c).astype(F32)
        order = lax.broadcasted_iota(jnp.int32, (HD // 2, 2 * TOK), 0).astype(F32)
        inverse = jnp.exp(order * F32(-LOG_BASE * 2.0 / HD))

        def body(d, carry):
            rows = pl.ds(pl.multiple_of(d * 2 * TOK, 2 * TOK), 2 * TOK)
            angles = inverse * pos_v[pl.ds(d, 1), :].astype(F32)
            cs, sn = jnp.cos(angles), jnp.sin(angles)
            cs = jnp.concatenate([cs, cs], axis=0).T
            sn = jnp.concatenate([sn, -sn], axis=0).T
            for head in range(QW // HD):
                cols = pl.ds(head * HD, HD)
                g = q_in[rows, cols].astype(F32)
                turned = g * cs + pltpu.roll(g, HD // 2, 1) * sn
                grads[d, :, :, cols] = turned.astype(BF16).reshape(2, TOK, HD)
            g = kv_own[rows, :].astype(F32) + kv_other[rows, :].astype(F32)
            cs, sn = cs * key + (1.0 - key), sn * key
            turned = g * cs + pltpu.roll(g, HD // 2, 1) * sn
            grads[d, :, :, pl.ds(QW, HD)] = turned.astype(BF16).reshape(2, TOK, HD)
            return carry

        lax.fori_loop(0, REP // (2 * TOK), body, 0)

    def transpose_all():
        def body(d, carry):
            cols = pl.ds(pl.multiple_of(d * 2 * TOK, 2 * TOK), 2 * TOK)
            grads_t[:, cols] = grads[d].reshape(2 * TOK, ROWS).T
            attn_t[:, cols] = attn_v[cols, :].T
            return carry

        lax.fori_loop(0, REP // (2 * TOK), body, 0)

    def hidden_partials(first, last):
        step = 512

        def body(i, carry):
            cols = pl.ds(pl.multiple_of(i * step, step), step)
            total = lax.dot_general(
                h_grads[...].reshape(REP // 2, 2 * ROWS), w_cat[cols, :],
                (((1,), (1,)), ((), ())), preferred_element_type=F32,
            )
            part_h[:, :, cols] = total.astype(BF16).reshape(2 * NY, TOK, step)
            return carry

        lax.fori_loop(first, last, body, 0)

    barrier = pltpu.get_barrier_semaphore()
    for device in partners:
        pl.semaphore_signal(barrier, inc=1, device_id=device, device_id_type=MESH)
    own_norm = load_own(normed, g_norm)
    l_pos = load(positions, pos_v)
    l_q = load(d_query, q_in)
    l_kv = load(d_keyvalue.at[:, pl.ds(pl.multiple_of(c * HD, HD), HD)], kv_own)
    l_attn = load(attn_out, attn_v)
    l_wq = load(w_query, w_cat.at[:, pl.ds(0, QW)])
    l_wkv = load(w_keyvalue, w_cat.at[:, pl.ds(QW, HD)])
    own_out = load_own(out_grad, g_out)
    pl.semaphore_wait(barrier, len(partners))

    steps = []
    for n, g, own in ((1, g_norm, own_norm), (2, g_out, own_out)):
        for phase in PHASES[n]:
            gather(g, own, phase, steps)
    finish_1 = reduce_dp(grads_t, g_norm, ct_q, sb_q, rb_q, xs_q, xr_q, steps)
    finish_2 = reduce_dp(attn_t, g_out, ct_o, sb_o, rb_o, xs_o, xr_o, steps)
    reduce_hidden(steps)
    held = {}

    def start():
        held["kv"] = send(
            d_keyvalue.at[:, pl.ds(pl.multiple_of((1 - c) * HD, HD), HD)], kv_other, dev_c
        )

    def weights():
        held["wq"] = send(w_query, w_cat.at[:, pl.ds(ROWS, QW)], dev_c)
        held["wkv"] = send(w_keyvalue, w_cat.at[:, pl.ds(ROWS + QW, HD)], dev_c)

    def rotate():
        for copy in (l_pos, l_q, l_kv):
            copy.wait()
        held["kv"].wait_recv()
        rotate_all()
        held["g"] = send(grads.at[:, 1 - c], h_grads.at[:, :, pl.ds(ROWS, ROWS)], dev_c)
        held["lg"] = load(grads.at[:, c], h_grads.at[:, :, pl.ds(0, ROWS)])

    def transpose():
        l_attn.wait()
        transpose_all()

    def hidden(i):
        if i == 0:
            for copy in (l_wq, l_wkv, held["lg"]):
                copy.wait()
            for name in ("wq", "wkv", "g"):
                held[name].wait_recv()
        hidden_partials(2 * i, 2 * i + 2)

    def finish_q():
        total = finish_1()
        query_out[...] = total[:QW].T.astype(BF16)
        keyvalue_out[...] = total[QW:].T.astype(BF16)

    def finish_o():
        out_out[...] = finish_2().astype(BF16)

    steps.extend((start, weights, rotate, transpose))
    steps.extend(functools.partial(hidden, i) for i in range(4))
    steps.extend((finish_q, finish_o))
    assert sorted(PLAN) == list(range(len(steps)))
    for at in PLAN:
        steps[at]()
    for message in messages:
        message.wait_send()


def place(*refs):
    for i in range(4):
        refs[4 + i][...] = refs[i][...]


def local(normed, out_grad, attn_out, d_query, d_keyvalue, positions, w_query, w_keyvalue):
    vmem = pltpu.VMEM
    shapes = (
        jax.ShapeDtypeStruct((TOK, D), BF16),
        jax.ShapeDtypeStruct((BLK, QW), BF16),
        jax.ShapeDtypeStruct((BLK, HD), BF16),
        jax.ShapeDtypeStruct((QW, BLK), BF16),
    )
    results = pl.pallas_call(
        kernel,
        out_shape=tuple(vmem(shape.shape, shape.dtype) for shape in shapes),
        in_specs=[pl.BlockSpec(memory_space=pl.ANY)] * 8,
        out_specs=[pl.BlockSpec(memory_space=vmem)] * 4,
        scratch_shapes=[
            vmem((SLOTS, REP, BLK), BF16),
            vmem((SLOTS, REP, BLK), BF16),
            vmem((D, 2 * ROWS), BF16),
            vmem((2 * NY, 2, TOK, ROWS), BF16),
            vmem((2 * NY, TOK, 2 * ROWS), BF16),
            vmem((ROWS, REP), BF16),
            vmem((REP, QW), BF16),
            vmem((QW, REP), BF16),
            vmem((REP, QW), BF16),
            vmem((REP, HD), BF16),
            vmem((REP, HD), BF16),
            vmem((8, REP // 8), jnp.int32),
            vmem((2 * NY, TOK, D), BF16),
            vmem((NY, TOK, HR_B), BF16),
            vmem((2, TOK, HR_A), BF16),
            vmem((TOK, HR_B1), BF16),
            vmem((TOK, HR_B - HR_B1), BF16),
            vmem((2, 2, TOK, HR_A), BF16),
            vmem((2, TOK, HR_B), BF16),
            vmem((TOK, HR_A), BF16),
            vmem((TOK, HR_A), BF16),
        ]
        + [
            shape
            for rows in (ROWS, QW)
            for shape in (
                vmem((7, 2, rows, BLK), BF16),
                vmem((2, rows, BLK), BF16),
                vmem((2, 4, 2, rows, BLK), BF16),
                vmem((rows, BLK), BF16),
                vmem((rows, BLK), BF16),
            )
        ]
        + [
            pltpu.SemaphoreType.DMA((SEMS,)),
            pltpu.SemaphoreType.DMA((SEMS,)),
            pltpu.SemaphoreType.DMA((LOCAL_SEMS,)),
        ],
        compiler_params=pltpu.CompilerParams(
            collective_id=0, has_side_effects=True, vmem_limit_bytes=60 * 1024 * 1024
        ),
    )(
        normed, out_grad, attn_out, d_query, d_keyvalue, positions.reshape(8, REP // 8),
        w_query, w_keyvalue,
    )
    return pl.pallas_call(
        place,
        out_shape=shapes,
        in_specs=[pl.BlockSpec(memory_space=vmem)] * 4,
        out_specs=[pl.BlockSpec(memory_space=vmem)] * 4,
    )(*(pltpu.with_memory_space_constraint(result, vmem) for result in results))


def solution(mesh):
    return jax.shard_map(
        local,
        mesh=mesh,
        in_specs=(
            P(("dp", "tensor"), None),
            P(("dp", "tensor"), None),
            P("dp", "tensor"),
            P("dp", "tensor"),
            P("dp", "tensor"),
            P("dp"),
            P(None, "tensor"),
            P(None, "tensor"),
        ),
        out_specs=(
            P(("dp", "tensor"), None),
            P("dp", "tensor"),
            P("dp", "tensor"),
            P("tensor", "dp"),
        ),
        check_vma=False,
    )
```

time: 124 us -> 100 us (0.81)
  the two profiles are of different devices: /device:TPU:48 before, /device:TPU:8 now
where the time goes in v2:
time: 100 us; the launch traced here: 98.7 us
  Pallas kernels  98.1 us (98%)
    pallas_call x1, Pallas kernels, local(): pl.pallas_call(kernel, out_shape=tuple((vmem(shape.shape, shape.dtype) fo...  97.1 us

profile of v2, /device:TPU:8, one launch (start us, length us, event | category | flops | bytes accessed | tf_op | source)
XLA Modules:
  0.0 98.7 jit_solution(17412620562394305604)
XLA Ops:
  0.6 97.1 %shard_map.111 = (bf16[64,4096]{1,0:T(8,128)(2,1)S(1)}, bf16[256,256]{1,0:T(8,128)(2,1)S(1)}, bf16[256,128]{1,0:T(8,128)(2,1)S(1)}, bf16[256,256]{1,0:T(8,128)(2,1)S(1)}) custom-call(bf16[64,4096]{1,0:T(8,128)(2,1)} %normed.1, bf16[64,4096]{1,0:T(8,128)(2,1)} %out_grad.1, bf16[1024,256]{1,0:T(8,128)(2,1)} %attn_out.1, bf16[1024,256]{1,0:T(8,128)(2,1)} %d_query.1, ...), custom_call_target="tpu_custom_call" | custom-call | tf_op jit(solution)/shard_map/pallas_call | solution.py:445
  97.8 0.9 shard_map.112

commit v3 on v2

--- a/solution.py
+++ b/solution.py
@@ -23,19 +23,20 @@
 NY = 4
 ORDER = (4, 3, -3, 2, -2, 1, -1, 0)
 SLOTS = 2 * NZ
-PHASES = {1: ((0, 5, 3), (8, 4, 4)), 2: ((0, 4, 4), (8, 5, 3))}
-HR_A = 2816
+PHASES = {1: ((0, 4, 4), (8, 5, 3)), 2: ((0, 3, 3), (6, 6, 4))}
+HR_A = 2560
 HR_B = D - HR_A
-HR_B1 = 640
+HR_B1 = 768
 SEMS = 160
+LAG = 30
 LOCAL_SEMS = 48
 
 PLAN = (
-    99, 0, 1, 100, 101, 2, 102, 3, 5, 4, 6, 12, 7, 8, 13, 103, 9, 104, 10, 105, 106, 14, 15, 17,
-    11, 48, 16, 49, 18, 24, 57, 50, 58, 51, 19, 25, 20, 21, 56, 59, 22, 23, 26, 27, 61, 52, 62,
-    53, 28, 29, 54, 30, 36, 60, 63, 55, 31, 37, 65, 33, 32, 66, 34, 38, 64, 67, 35, 69, 70, 39,
-    78, 40, 71, 42, 41, 90, 79, 72, 43, 91, 68, 44, 45, 77, 46, 80, 47, 73, 82, 92, 83, 74, 75,
-    76, 81, 84, 94, 93, 86, 87, 96, 85, 88, 89, 95, 97, 107, 108, 98,
+    100, 0, 1, 101, 102, 2, 3, 103, 5, 4, 6, 12, 13, 7, 9, 8, 104, 14, 105, 106, 107, 15, 16, 10,
+    18, 17, 24, 25, 11, 48, 19, 49, 20, 57, 21, 50, 58, 51, 26, 27, 36, 28, 56, 22, 29, 59, 30,
+    37, 23, 52, 53, 31, 32, 33, 61, 62, 54, 55, 38, 60, 39, 63, 41, 40, 65, 66, 34, 42, 90, 35,
+    69, 64, 67, 70, 43, 91, 44, 78, 71, 45, 79, 46, 77, 47, 80, 72, 73, 92, 74, 75, 76, 68, 94,
+    93, 82, 83, 81, 84, 96, 86, 87, 95, 97, 85, 88, 108, 89, 99, 98, 109,
 )
 
 
@@ -91,11 +92,12 @@
     def columns(j, hh):
         return pl.ds(pl.multiple_of((hh * NZ + (z + NZ + ORDER[j]) % NZ) * BLK, BLK), BLK)
 
-    def load_own(src, g):
+    def load_own(src, g, own, first, last):
         rows = pl.ds(pl.multiple_of(tensor * TOK, TOK), TOK)
-        return [
-            load(src.at[:, columns(i // 2, i % 2)], g.at[i, rows, :]) for i in range(SLOTS)
-        ]
+        own.extend(
+            load(src.at[:, columns(i // 2, i % 2)], g.at[i, rows, :])
+            for i in range(first, last)
+        )
 
     def gather(g, own, phase, steps):
         first, count_a, count_b = phase
@@ -297,21 +299,26 @@
             ).astype(BF16)
             m["HX1"] = send(hs_a, rx_a, dev_x)
 
-        def hr5():
+        def hr5b():
             d = at(x, y)
             m["HX0", 3].wait_recv()
-            for name in ("HP2a", "HM2a", "HP3", "HM3", "HX1"):
+            m["HP3"].wait_recv()
+            m["HM3"].wait_recv()
+            hidden_out[:, cb] = (
+                (p[d, :, cb].astype(F32) + rx_b[3].astype(F32))
+                + (ry_b[0].astype(F32) + ry_b[1].astype(F32))
+            ).astype(BF16)
+
+        def hr5a():
+            d = at(x, y)
+            for name in ("HP2a", "HM2a", "HX1"):
                 m[name].wait_recv()
             hidden_out[:, ca] = (
                 (p[d, :, ca].astype(F32) + ry_a[0, 0].astype(F32))
                 + (ry_a[1, 0].astype(F32) + rx_a[...].astype(F32))
             ).astype(BF16)
-            hidden_out[:, cb] = (
-                (p[d, :, cb].astype(F32) + rx_b[3].astype(F32))
-                + (ry_b[0].astype(F32) + ry_b[1].astype(F32))
-            ).astype(BF16)
-
-        steps.extend((hr0x, hr0, hr1, hr2m, hr2p, hr3p, hr3m, hr4, hr5))
+
+        steps.extend((hr0x, hr0, hr1, hr2m, hr2p, hr3p, hr3m, hr4, hr5b, hr5a))
 
     def rotate_all():
         key = (1 - c).astype(F32)
@@ -363,15 +370,8 @@
     barrier = pltpu.get_barrier_semaphore()
     for device in partners:
         pl.semaphore_signal(barrier, inc=1, device_id=device, device_id_type=MESH)
-    own_norm = load_own(normed, g_norm)
-    l_pos = load(positions, pos_v)
-    l_q = load(d_query, q_in)
-    l_kv = load(d_keyvalue.at[:, pl.ds(pl.multiple_of(c * HD, HD), HD)], kv_own)
-    l_attn = load(attn_out, attn_v)
-    l_wq = load(w_query, w_cat.at[:, pl.ds(0, QW)])
-    l_wkv = load(w_keyvalue, w_cat.at[:, pl.ds(QW, HD)])
-    own_out = load_own(out_grad, g_out)
-    pl.semaphore_wait(barrier, len(partners))
+    own_norm, own_out, held = [], [], {}
+    load_own(normed, g_norm, own_norm, 0, SLOTS // 2)
 
     steps = []
     for n, g, own in ((1, g_norm, own_norm), (2, g_out, own_out)):
@@ -380,33 +380,40 @@
     finish_1 = reduce_dp(grads_t, g_norm, ct_q, sb_q, rb_q, xs_q, xr_q, steps)
     finish_2 = reduce_dp(attn_t, g_out, ct_o, sb_o, rb_o, xs_o, xr_o, steps)
     reduce_hidden(steps)
-    held = {}
-
     def start():
+        pl.semaphore_wait(barrier, len(partners))
+
+    def weights():
+        held["lkv"] = load(d_keyvalue.at[:, pl.ds(pl.multiple_of(c * HD, HD), HD)], kv_own)
         held["kv"] = send(
             d_keyvalue.at[:, pl.ds(pl.multiple_of((1 - c) * HD, HD), HD)], kv_other, dev_c
         )
-
-    def weights():
+        held["lpos"] = load(positions, pos_v)
+        held["lq"] = load(d_query, q_in)
+        load_own(normed, g_norm, own_norm, SLOTS // 2, SLOTS)
+        held["lattn"] = load(attn_out, attn_v)
+        held["lwq"] = load(w_query, w_cat.at[:, pl.ds(0, QW)])
+        held["lwkv"] = load(w_keyvalue, w_cat.at[:, pl.ds(QW, HD)])
         held["wq"] = send(w_query, w_cat.at[:, pl.ds(ROWS, QW)], dev_c)
         held["wkv"] = send(w_keyvalue, w_cat.at[:, pl.ds(ROWS + QW, HD)], dev_c)
+        load_own(out_grad, g_out, own_out, 0, SLOTS)
 
     def rotate():
-        for copy in (l_pos, l_q, l_kv):
-            copy.wait()
+        for name in ("lpos", "lq", "lkv"):
+            held[name].wait()
         held["kv"].wait_recv()
         rotate_all()
         held["g"] = send(grads.at[:, 1 - c], h_grads.at[:, :, pl.ds(ROWS, ROWS)], dev_c)
         held["lg"] = load(grads.at[:, c], h_grads.at[:, :, pl.ds(0, ROWS)])
 
     def transpose():
-        l_attn.wait()
+        held["lattn"].wait()
         transpose_all()
 
     def hidden(i):
         if i == 0:
-            for copy in (l_wq, l_wkv, held["lg"]):
-                copy.wait()
+            for name in ("lwq", "lwkv", "lg"):
+                held[name].wait()
             for name in ("wq", "wkv", "g"):
                 held[name].wait_recv()
         hidden_partials(2 * i, 2 * i + 2)
@@ -423,9 +430,16 @@
     steps.extend(functools.partial(hidden, i) for i in range(4))
     steps.extend((finish_q, finish_o))
     assert sorted(PLAN) == list(range(len(steps)))
+    issued = []
+    waited = 0
     for at in PLAN:
         steps[at]()
-    for message in messages:
+        issued.append(len(messages))
+        if len(issued) > LAG:
+            for message in messages[waited:issued[-1 - LAG]]:
+                message.wait_send()
+            waited = issued[-1 - LAG]
+    for message in messages[waited:]:
         message.wait_send()
 
 

time: 100 us -> 97.5 us (0.975); the launches traced: 98.7 us -> 97.4 us
  Pallas kernels: 98.1 us -> 96.7 us
    pallas_call x1, Pallas kernels: 97.1 us -> 95.8 us  [local(): pl.pallas_call(kernel, out_shape=tuple((vmem(shape.shape, shape.dtype) fo...]
where the time goes in v3:
time: 97.5 us; the launch traced here: 97.4 us
  Pallas kernels  96.7 us (99%)
    pallas_call x1, Pallas kernels, local(): pl.pallas_call(kernel, out_shape=tuple((vmem(shape.shape, shape.dtype) fo...  95.8 us

profile of v3, /device:TPU:8, one launch (start us, length us, event | category | flops | bytes accessed | tf_op | source)
XLA Modules:
  0.0 97.4 jit_solution(12110142322993460886)
XLA Ops:
  0.6 95.8 %shard_map.111 = (bf16[64,4096]{1,0:T(8,128)(2,1)S(1)}, bf16[256,256]{1,0:T(8,128)(2,1)S(1)}, bf16[256,128]{1,0:T(8,128)(2,1)S(1)}, bf16[256,256]{1,0:T(8,128)(2,1)S(1)}) custom-call(bf16[64,4096]{1,0:T(8,128)(2,1)} %normed.1, bf16[64,4096]{1,0:T(8,128)(2,1)} %out_grad.1, bf16[1024,256]{1,0:T(8,128)(2,1)} %attn_out.1, bf16[1024,256]{1,0:T(8,128)(2,1)} %d_query.1, ...), custom_call_target="tpu_custom_call" | custom-call | tf_op jit(solution)/shard_map/pallas_call | solution.py:459
  96.4 0.9 shard_map.112

commit v4 on v3

--- a/solution.py
+++ b/solution.py
@@ -23,7 +23,7 @@
 NY = 4
 ORDER = (4, 3, -3, 2, -2, 1, -1, 0)
 SLOTS = 2 * NZ
-PHASES = {1: ((0, 4, 4), (8, 5, 3)), 2: ((0, 3, 3), (6, 6, 4))}
+PHASES = {1: ((0, 4, 4), (8, 5, 3)), 2: ((0, 2, 2), (4, 7, 5))}
 HR_A = 2560
 HR_B = D - HR_A
 HR_B1 = 768
@@ -32,11 +32,11 @@
 LOCAL_SEMS = 48
 
 PLAN = (
-    100, 0, 1, 101, 102, 2, 3, 103, 5, 4, 6, 12, 13, 7, 9, 8, 104, 14, 105, 106, 107, 15, 16, 10,
-    18, 17, 24, 25, 11, 48, 19, 49, 20, 57, 21, 50, 58, 51, 26, 27, 36, 28, 56, 22, 29, 59, 30,
-    37, 23, 52, 53, 31, 32, 33, 61, 62, 54, 55, 38, 60, 39, 63, 41, 40, 65, 66, 34, 42, 90, 35,
-    69, 64, 67, 70, 43, 91, 44, 78, 71, 45, 79, 46, 77, 47, 80, 72, 73, 92, 74, 75, 76, 68, 94,
-    93, 82, 83, 81, 84, 96, 86, 87, 95, 97, 85, 88, 108, 89, 99, 98, 109,
+    100, 0, 1, 101, 102, 2, 3, 103, 5, 4, 6, 12, 13, 7, 9, 8, 104, 14, 105, 106, 107, 15, 24, 10,
+    16, 25, 18, 17, 11, 48, 49, 57, 50, 19, 58, 51, 20, 21, 26, 27, 29, 36, 28, 37, 59, 56, 22,
+    30, 31, 32, 33, 23, 61, 52, 62, 53, 54, 38, 55, 60, 39, 63, 41, 40, 65, 66, 34, 42, 90, 64,
+    35, 67, 69, 70, 78, 43, 91, 44, 45, 46, 68, 47, 71, 79, 72, 80, 77, 92, 76, 74, 73, 82, 93,
+    94, 75, 83, 81, 84, 96, 86, 87, 85, 97, 95, 88, 108, 89, 98, 99, 109,
 )
 
 
@@ -46,7 +46,7 @@
     g_norm, g_out, w_cat, grads, h_grads, grads_t, attn_v, attn_t, q_in, kv_own, kv_other,
     pos_v, part_h, rx_b, r2_a, r2_b1, r2_b2, ry_a, ry_b, rx_a, hs_a,
     ct_q, sb_q, rb_q, xs_q, xr_q, ct_o, sb_o, rb_o, xs_o, xr_o,
-    send_sems, recv_sems, local_sems,
+    send_sems, recv_sems, local_sems, ready_z, ready_h,
 ):
     dp = lax.axis_index("dp")
     tensor = lax.axis_index("tensor")
@@ -68,7 +68,10 @@
     dev_zp = (h * NZ + (z + 1) % NZ, tensor)
     dev_zm = (h * NZ + (z + NZ - 1) % NZ, tensor)
     dev_h = ((1 - h) * NZ + z, tensor)
-    partners = (dev_x, dev_yp, dev_ym, dev_c, dev_zp, dev_zm, dev_h)
+
+    def signal(sem, *devices):
+        for device in devices:
+            pl.semaphore_signal(sem, inc=1, device_id=device, device_id_type=MESH)
 
     messages = []
     locals_ = []
@@ -180,7 +183,7 @@
 
         steps.extend((ownx, own_y, p0, x0, p1, x1, p2, p3, c6, c4, c7, done))
 
-    def reduce_dp(lhs, g, ct, sb, rb, xs, xr, steps):
+    def reduce_dp(lhs, g, ct, sb, rb, xs, xr, steps, reach):
         m = {}
 
         def product(i):
@@ -188,6 +191,7 @@
 
         def first():
             sb[0] = product(0)
+            reach()
             m["P1", 0] = send(sb.at[0], rb.at[0, 0, 0], dev_zp)
             sb[1] = product(1)
             m["M1", 1] = send(sb.at[1], rb.at[1, 0, 1], dev_zm)
@@ -368,20 +372,27 @@
         lax.fori_loop(first, last, body, 0)
 
     barrier = pltpu.get_barrier_semaphore()
-    for device in partners:
-        pl.semaphore_signal(barrier, inc=1, device_id=device, device_id_type=MESH)
+    signal(barrier, dev_x, dev_yp, dev_ym, dev_c)
+    pl.when(z % 2 == 0)(lambda: signal(barrier, dev_zp, dev_zm))
+    pl.when(h == 0)(lambda: signal(barrier, dev_h))
     own_norm, own_out, held = [], [], {}
     load_own(normed, g_norm, own_norm, 0, SLOTS // 2)
+
+    def reach_dp():
+        pl.when(z % 2 == 0)(lambda: pl.semaphore_wait(ready_z, 2))
+        pl.when(h == 0)(lambda: pl.semaphore_wait(ready_h, 1))
 
     steps = []
     for n, g, own in ((1, g_norm, own_norm), (2, g_out, own_out)):
         for phase in PHASES[n]:
             gather(g, own, phase, steps)
-    finish_1 = reduce_dp(grads_t, g_norm, ct_q, sb_q, rb_q, xs_q, xr_q, steps)
-    finish_2 = reduce_dp(attn_t, g_out, ct_o, sb_o, rb_o, xs_o, xr_o, steps)
+    finish_1 = reduce_dp(grads_t, g_norm, ct_q, sb_q, rb_q, xs_q, xr_q, steps, reach_dp)
+    finish_2 = reduce_dp(attn_t, g_out, ct_o, sb_o, rb_o, xs_o, xr_o, steps, lambda: None)
     reduce_hidden(steps)
     def start():
-        pl.semaphore_wait(barrier, len(partners))
+        pl.semaphore_wait(barrier, 4 + 2 * (z % 2) + h)
+        pl.when(z % 2 == 1)(lambda: signal(ready_z, dev_zp, dev_zm))
+        pl.when(h == 1)(lambda: signal(ready_h, dev_h))
 
     def weights():
         held["lkv"] = load(d_keyvalue.at[:, pl.ds(pl.multiple_of(c * HD, HD), HD)], kv_own)
@@ -499,6 +510,8 @@
             pltpu.SemaphoreType.DMA((SEMS,)),
             pltpu.SemaphoreType.DMA((SEMS,)),
             pltpu.SemaphoreType.DMA((LOCAL_SEMS,)),
+            pltpu.SemaphoreType.REGULAR,
+            pltpu.SemaphoreType.REGULAR,
         ],
         compiler_params=pltpu.CompilerParams(
             collective_id=0, has_side_effects=True, vmem_limit_bytes=60 * 1024 * 1024

time: 97.5 us -> 95.8 us (0.983); the launches traced: 97.4 us -> 94.7 us
  Pallas kernels: 96.7 us -> 94.1 us
    pallas_call x1, Pallas kernels: 95.8 us -> 93.1 us  [local(): pl.pallas_call(kernel, out_shape=tuple((vmem(shape.shape, shape.dtype) fo...]
where the time goes in v4:
time: 95.8 us; the launch traced here: 94.7 us
  Pallas kernels  94.1 us (98%)
    pallas_call x1, Pallas kernels, local(): pl.pallas_call(kernel, out_shape=tuple((vmem(shape.shape, shape.dtype) fo...  93.1 us

profile of v4, /device:TPU:8, one launch (start us, length us, event | category | flops | bytes accessed | tf_op | source)
XLA Modules:
  0.0 94.7 jit_solution(6693522298511310911)
XLA Ops:
  0.6 93.1 %shard_map.111 = (bf16[64,4096]{1,0:T(8,128)(2,1)S(1)}, bf16[256,256]{1,0:T(8,128)(2,1)S(1)}, bf16[256,128]{1,0:T(8,128)(2,1)S(1)}, bf16[256,256]{1,0:T(8,128)(2,1)S(1)}) custom-call(bf16[64,4096]{1,0:T(8,128)(2,1)} %normed.1, bf16[64,4096]{1,0:T(8,128)(2,1)} %out_grad.1, bf16[1024,256]{1,0:T(8,128)(2,1)} %attn_out.1, bf16[1024,256]{1,0:T(8,128)(2,1)} %d_query.1, ...), custom_call_target="tpu_custom_call" | custom-call | tf_op jit(solution)/shard_map/pallas_call | solution.py:470
  93.7 0.9 %shard_map.112 = (bf16[64,4096]{1,0:T(8,128)(2,1)}, bf16[256,256]{1,0:T(8,128)(2,1)}, bf16[256,128]{1,0:T(8,128)(2,1)}, bf16[256,256]{1,0:T(8,128)(2,1)}) custom-call(bf16[64,4096]{1,0:T(8,128)(2,1)S(1)} %get-tuple-element.8.refs_0_, bf16[256,256]{1,0:T(8,128)(2,1)S(1)} %get-tuple-element.9.refs_1_, bf16[256,128]{1,0:T(8,128)(2,1)S(1)} %get-tuple-element.10.refs_2_, ...), custom_call_target="tpu_custom_call" | custom-call | tf_op jit(solution)/shard_map/pallas_call | solution.py:523

commit v5 on v4

--- a/solution.py
+++ b/solution.py
@@ -28,7 +28,7 @@
 HR_B = D - HR_A
 HR_B1 = 768
 SEMS = 160
-LAG = 30
+LAG = 48
 LOCAL_SEMS = 48
 
 PLAN = (

time: 95.8 us -> 95.8 us (level)
  no operation moved by 1% of the time
where the time goes in v5:
time: 95.8 us; the launch traced here: 94.8 us
  Pallas kernels  94.1 us (98%)
    pallas_call x1, Pallas kernels, local(): pl.pallas_call(kernel, out_shape=tuple((vmem(shape.shape, shape.dtype) fo...  93.2 us

profile of v5, /device:TPU:8, one launch (start us, length us, event | category | flops | bytes accessed | tf_op | source)
XLA Modules:
  0.0 94.8 jit_solution(8313632525270971168)
XLA Ops:
  0.6 93.2 %shard_map.111 = (bf16[64,4096]{1,0:T(8,128)(2,1)S(1)}, bf16[256,256]{1,0:T(8,128)(2,1)S(1)}, bf16[256,128]{1,0:T(8,128)(2,1)S(1)}, bf16[256,256]{1,0:T(8,128)(2,1)S(1)}) custom-call(bf16[64,4096]{1,0:T(8,128)(2,1)} %normed.1, bf16[64,4096]{1,0:T(8,128)(2,1)} %out_grad.1, bf16[1024,256]{1,0:T(8,128)(2,1)} %attn_out.1, bf16[1024,256]{1,0:T(8,128)(2,1)} %d_query.1, ...), custom_call_target="tpu_custom_call" | custom-call | tf_op jit(solution)/shard_map/pallas_call | solution.py:470
  93.8 0.9 %shard_map.112 = (bf16[64,4096]{1,0:T(8,128)(2,1)}, bf16[256,256]{1,0:T(8,128)(2,1)}, bf16[256,128]{1,0:T(8,128)(2,1)}, bf16[256,256]{1,0:T(8,128)(2,1)}) custom-call(bf16[64,4096]{1,0:T(8,128)(2,1)S(1)} %get-tuple-element.8.refs_0_, bf16[256,256]{1,0:T(8,128)(2,1)S(1)} %get-tuple-element.9.refs_1_, bf16[256,128]{1,0:T(8,128)(2,1)S(1)} %get-tuple-element.10.refs_2_, ...), custom_call_target="tpu_custom_call" | custom-call | tf_op jit(solution)/shard_map/pallas_call | solution.py:523
